TPU v7x, 32 devices: a whole 2x2x4 slice. The times are simulated.
32 devices in a mesh: lat: 4 (over y, core), grp: 8 (over z, x).
Axes of the slice: x: 2, y: 2, z: 4, core: 2. Of those that a mesh axis runs over, the one named last changes fastest.
Arguments:
- inputs: bfloat16 [256, 1024, 1024], P(None, ('lat', 'grp')), may hold values from -6 to 6
- w_in: bfloat16 [256, 512], replicated, may hold values from -0.375 to 0.375
- bias_in: float32 [512], replicated, may hold values from -3 to 3
- w_out: bfloat16 [512, 256], replicated, may hold values from -0.25 to 0.25
- advected: bfloat16 [256, 1024, 1024], P('grp', 'lat'), may hold values from -6 to 6
- cotangent: bfloat16 [256, 1024, 1024], P('grp', 'lat'), may hold values from -6 to 6
- offsets: int32 [2, 64, 4], P(None, 'lat'), may hold values from 0 to 3
- stencil_row: int32 [64, 4], P('lat'), may hold values from 0 to 4
- stencil_col: int32 [64, 4], P('lat'), may hold values from 0 to 124
- fracs: float32 [2, 64, 4], P(None, 'lat'), may hold values from 0 to 1
Outputs:
- grad_inputs: bfloat16 [256, 1024, 1024], P(None, ('lat', 'grp'))
- grad_w_in: float32 [256, 512], P(None, ('lat', 'grp'))
- grad_bias: float32 [512], P(('lat', 'grp'))
- grad_w_out: float32 [512, 256], P(('lat', 'grp'))
- grad_frac: float32 [2, 64, 4], P(None, 'lat')
All inputs are finite; a program needn't handle non-finite values.
Results may differ from a plain program's by a relative error of at most 0.0068.
Values may be sent and summed in bfloat16 or wider, within the bound.
A program may use at most 256 MiB of HBM per device.

v0:
```python
import math

import jax
import jax.numpy as jnp
from jax import lax
from jax.sharding import PartitionSpec as P

C = 256
BH = 16
BW = 256


def extended_2(cells, sides, width):
    for axis, dim in sides:
        count = lax.axis_size(axis)
        ends = count - 1
        head = lax.slice_in_dim(cells, 0, width, axis=dim)
        tail = lax.slice_in_dim(cells, cells.shape[dim] - width, cells.shape[dim], axis=dim)
        cells = jnp.concatenate(
            [
                lax.ppermute(tail, axis, [(i, (i + 1) % count) for i in range(ends)]),
                cells,
                lax.ppermute(head, axis, [((i + 1) % count, i) for i in range(ends)]),
            ],
            axis=dim,
        )
    return cells


def from_behind(block, axis, distance):
    devices = range(lax.axis_size(axis))
    route = [(i - distance, i) for i in devices if i - distance in devices]
    return lax.ppermute(block, axis, route)


def catmull(frac):
    square = frac * frac
    cube = square * frac
    weights = (
        0.5 * (-cube + 2.0 * square - frac),
        0.5 * (3.0 * cube - 5.0 * square + 2.0),
        0.5 * (-3.0 * cube + 4.0 * square + frac),
        0.5 * (cube - square),
    )
    slopes = (
        0.5 * (-3.0 * square + 4.0 * frac - 1.0),
        0.5 * (9.0 * square - 10.0 * frac),
        0.5 * (-9.0 * square + 8.0 * frac + 1.0),
        0.5 * (3.0 * square - 2.0 * frac),
    )
    return (weights, slopes)


def band_matrix(position, frac, inner):
    offset_grid = (
        jnp.arange(3 * inner, dtype=jnp.int32)[None, None, :]
        - jnp.arange(inner, dtype=jnp.int32)[None, :, None]
        - position[:, None, None]
    )
    weights, slopes = catmull(frac)
    value = jnp.zeros(offset_grid.shape, jnp.float32)
    slope = jnp.zeros(offset_grid.shape, jnp.float32)
    for tap in range(4):
        value = value + jnp.where(offset_grid == tap, weights[tap][:, None, None], 0.0)
        slope = slope + jnp.where(offset_grid == tap, slopes[tap][:, None, None], 0.0)
    return (value.astype(jnp.bfloat16), slope.astype(jnp.bfloat16))


def contract_points(left, right):
    return lax.dot_general(
        left, right, (((1,), (1,)), ((), ())), preferred_element_type=jnp.float32
    )


def shards(
    inputs, w_in, bias_in, w_out, advected, cotangent, offsets, stencil_row, stencil_col, fracs
):
    channels_dev, band_rows, columns = advected.shape
    row_blocks = band_rows // BH
    blocks = columns // BW
    point_rows = inputs.shape[1]
    x_flat = inputs.reshape(C, point_rows * columns)
    pre_act = (
        lax.dot_general(w_in, x_flat, (((0,), (0,)), ((), ())), preferred_element_type=jnp.float32)
        + bias_in[:, None]
    )
    sigma = jax.nn.sigmoid(pre_act)
    act = (pre_act * sigma).astype(jnp.bfloat16)
    padded = extended_2(advected, (("lat", 1),), BH)
    row_pos = BH // 2 * offsets[0] + stencil_row
    col_pos = BW // 2 * offsets[1] + stencil_col

    def per_row(index, state):
        extended, frac_acc = state
        drow = lax.dynamic_slice_in_dim(cotangent, index * BH, BH, 1)
        window = lax.dynamic_slice_in_dim(padded, index * BH, 3 * BH, 1)
        ry_value, ry_slope = band_matrix(row_pos[index], fracs[0][index], BH)
        rx_value, rx_slope = band_matrix(col_pos[index], fracs[1][index], BW)
        column_sums = [
            jnp.zeros((channels_dev, 3 * BH, BW), jnp.float32) for unused in range(blocks)
        ]
        grad_rows = []
        grad_cols = []
        for block in range(blocks):
            left = (block - 1) % blocks
            right = (block + 1) % blocks
            rx_both = jnp.concatenate([rx_value[block], rx_slope[block]], axis=1)
            block_cot = drow[:, :, block * BW : (block + 1) * BW].reshape(channels_dev * BH, BW)
            product = jnp.dot(block_cot, rx_both, preferred_element_type=jnp.float32)
            product = product.reshape(channels_dev, BH, 6 * BW)
            z_value = product[:, :, : 3 * BW]
            z_slope = product[:, :, 3 * BW :]
            ry_value_all = jnp.broadcast_to(ry_value[block], (channels_dev, BH, 3 * BH))
            ry_slope_all = jnp.broadcast_to(ry_slope[block], (channels_dev, BH, 3 * BH))
            spread = jnp.einsum(
                "cho,chv->cov",
                ry_value_all,
                z_value.astype(jnp.bfloat16),
                preferred_element_type=jnp.float32,
            )
            source = jnp.concatenate(
                [
                    window[:, :, left * BW : (left + 1) * BW],
                    window[:, :, block * BW : (block + 1) * BW],
                    window[:, :, right * BW : (right + 1) * BW],
                ],
                axis=2,
            )
            ry_both = jnp.concatenate([ry_value_all, ry_slope_all], axis=1)
            lifted = jnp.einsum("cjo,cov->cjv", ry_both, source, preferred_element_type=jnp.float32)
            grad_rows.append(jnp.sum(lifted[:, BH:] * z_value))
            grad_cols.append(jnp.sum(lifted[:, :BH] * z_slope))
            for part, target in ((0, left), (1, block), (2, right)):
                column_sums[target] = (
                    column_sums[target] + spread[:, :, part * BW : (part + 1) * BW]
                )
        row_sum = jnp.concatenate(column_sums, axis=2)
        current = lax.dynamic_slice_in_dim(extended, index * BH, 3 * BH, 1)
        extended = lax.dynamic_update_slice_in_dim(extended, current + row_sum, index * BH, 1)
        frac_acc = frac_acc.at[:, index].set(
            jnp.stack([jnp.stack(grad_rows), jnp.stack(grad_cols)])
        )
        return (extended, frac_acc)

    start_field = jnp.zeros((channels_dev, band_rows + 2 * BH, columns), jnp.float32)
    start_frac = jnp.zeros((2, row_blocks, blocks), jnp.float32)
    extended, frac_local = lax.fori_loop(0, row_blocks, per_row, (start_field, start_frac))
    from_below = from_behind(extended[:, :BH], "lat", -1)
    from_above = from_behind(extended[:, band_rows + BH :], "lat", 1)
    inner_rows = jnp.concatenate(
        [
            extended[:, BH : 2 * BH] + from_above,
            extended[:, 2 * BH : band_rows],
            extended[:, band_rows : band_rows + BH] + from_below,
        ],
        axis=1,
    )
    dy_band = inner_rows.astype(jnp.bfloat16)
    dy_points = lax.all_to_all(dy_band, "grp", split_axis=1, concat_axis=0, tiled=True)
    dy_flat = dy_points.reshape(C, point_rows * columns)
    dact = jnp.dot(w_out, dy_flat, preferred_element_type=jnp.float32)
    frac_total = lax.psum(frac_local, "grp")
    grad_frac = frac_total / math.sqrt(C * BH * BW)
    dpre = (dact * sigma * (1.0 + pre_act * (1.0 - sigma))).astype(jnp.bfloat16)
    dx_flat = dy_flat.astype(jnp.float32) + jnp.dot(w_in, dpre, preferred_element_type=jnp.float32)
    grad_inputs = dx_flat.astype(jnp.bfloat16).reshape(C, point_rows, columns)
    grad_first = contract_points(x_flat, dpre)
    grad_shift = jnp.sum(dpre.astype(jnp.float32), axis=1)
    grad_second = contract_points(act, dy_flat)
    total_points = point_rows * columns * lax.axis_size("lat") * lax.axis_size("grp")
    scale = 1.0 / math.sqrt(total_points)
    banded = (
        lax.psum_scatter(grad_first, "lat", scatter_dimension=1, tiled=True),
        lax.psum_scatter(grad_shift, "lat", scatter_dimension=0, tiled=True),
        lax.psum_scatter(grad_second, "lat", scatter_dimension=0, tiled=True),
    )
    summed = (
        lax.psum_scatter(banded[0], "grp", scatter_dimension=1, tiled=True),
        lax.psum_scatter(banded[1], "grp", scatter_dimension=0, tiled=True),
        lax.psum_scatter(banded[2], "grp", scatter_dimension=0, tiled=True),
    )
    return (grad_inputs, summed[0] * scale, summed[1] * scale, summed[2] * scale, grad_frac)


def solution(mesh):
    placed = (
        P(None, ("lat", "grp"), None),
        P(),
        P(),
        P(),
        P("grp", "lat", None),
        P("grp", "lat", None),
        P(None, "lat", None),
        P("lat", None),
        P("lat", None),
        P(None, "lat", None),
    )
    return jax.shard_map(
        shards,
        mesh=mesh,
        in_specs=placed,
        out_specs=(
            P(None, ("lat", "grp"), None),
            P(None, ("lat", "grp")),
            P(("lat", "grp")),
            P(("lat", "grp"), None),
            P(None, "lat", None),
        ),
        check_vma=False,
    )
```

profile of v0, /device:TPU:0, one launch (start us, length us, event | category | flops | bytes accessed | tf_op | source)
XLA Modules:
  0.0 1594.4 jit_solution(8253238335614168965)
XLA Ops:
  19.1 18.6 %pad_maximum_fusion = bf16[32,288,1024]{2,1,0:T(8,128)(2,1)} fusion(bf16[32,16,1024]{2,1,0:T(8,128)(2,1)S(1)} %collective-permute-done.1, bf16[32,256,1024]{2,1,0:T(8,128)(2,1)} %param.18, bf16[32,16,1024]{2,1,0:T(8,128)(2,1)S(1)} %collective-permute-done), kind=kLoop, calls=%fused_computation.201 | loop fusion | flops 56623104 | bytes 37748736 | tf_op jit(solution)/shard_map/concatenate | solution.py:19
  37.7 12.7 broadcast_in_dim.522.clone
  50.4 855.0 %while.19 = (s32[]{:T(128)}, f32[32,288,1024]{2,0,1:T(8,128)}, f32[2,16,4]{2,0,1:T(2,128)S(1)}, s32[16,4]{1,0:T(8,128)S(1)}, f32[2,16,4]{2,1,0:T(8,128)S(1)}, /*...) while((s32[]{:T(128)}, f32[32,288,1024]{2,0,1:T(8,128)}, ...), condition=%wide.region_10.11_spmd, body=%wide.region_0.10_spmd.sunk | while | flops 2112618496 | bytes 176499824 | solution.py:147
  103.6 7.1 maximum_add_fusion.2
  156.1 7.1 maximum_add_fusion.2
  208.6 7.1 maximum_add_fusion.2
  261.2 7.1 maximum_add_fusion.2
  313.7 7.1 maximum_add_fusion.2
  366.3 7.1 maximum_add_fusion.2
  418.8 7.1 maximum_add_fusion.2
  471.3 7.1 maximum_add_fusion.2
  523.8 7.1 maximum_add_fusion.2
  576.4 7.1 maximum_add_fusion.2
  628.9 7.1 maximum_add_fusion.2
  891.6 7.1 maximum_add_fusion.2
  908.0 14.1 collective-permute-start.2
  923.4 10.8 slice.820
  937.2 7.4 pad_maximum_fusion.1
  950.4 18.7 %copy.49 = bf16[32,8,32,1024]{3,1,2,0:T(8,128)(2,1)} copy(bf16[32,8,32,1024]{3,2,1,0:T(8,128)(2,1)} %bitcast.156) | data formatting | bytes 33554432
  969.1 28.8 %fusion.118 = f32[512,32768]{0,1:T(8,128)} fusion(bf16[256,512]{1,0:T(8,128)(2,1)S(1)} %copy-done, bf16[256,32768]{1,0:T(8,128)(2,1)} %bitcast.150), kind=kOutput, calls=%fused_computation.216 | convolution fusion | flops 8589934592 | bytes 84148224 | tf_op jit(solution)/shard_map/dot_general | solution.py:84
  997.9 303.3 %all-to-all-done = bf16[32,256,1024]{2,0,1:T(8,128)(2,1)} async-done(((bf16[32,256,1024]{2,0,1:T(8,128)(2,1)}), bf16[32,256,1024]{2,0,1:T(8,128)(2,1)}, u32[]{:S(2)}, u32[]{:S(2)}) %all-to-all-start) | async-done | bytes 16777248 | tf_op jit(solution)/shard_map/all_to_all | solution.py:159
  1301.2 15.3 copy.38
  1316.5 11.2 copy.48
  1327.7 47.1 %convert_reduce_fusion = (f32[512]{0:T(512)}, bf16[512,32768]{0,1:T(8,128)(2,1)}) fusion(f32[512,32768]{0,1:T(8,128)} %fusion.118, f32[512]{0:T(512)S(1)} %copy-done.10, bf16[256,32768]{1,0:T(8,128)(2,1)} %bitcast.152, bf16[512,256]{1,0:T(8,128)(2,1)S(1)} %copy-done.9), kind=kOutput, calls=%fused_computation.194 | convolution fusion | flops 8791261184 | bytes 117706752 | tf_op jit(solution)/shard_map/dot_general | solution.py:161
  1374.8 19.5 %convolution_bitcast_fusion.1 = f32[256,512]{0,1:T(8,128)} fusion(bf16[512,32768]{0,1:T(8,128)(2,1)} %get-tuple-element.376, bf16[256,32768]{1,0:T(8,128)(2,1)} %bitcast.151), kind=kOutput, calls=%fused_computation.205 | convolution fusion | flops 8589934592 | bytes 50855936 | tf_op jit(solution)/shard_map/dot_general | solution.py:70
  1394.4 31.0 %fusion.111 = f32[512,256]{1,0:T(8,128)} fusion(bf16[256,32768]{1,0:T(8,128)(2,1)} %bitcast.153, f32[512,32768]{0,1:T(8,128)} %fusion.118, f32[512]{0:T(512)S(1)} %copy-done.10), kind=kOutput, calls=%fused_computation.199 | convolution fusion | flops 8690597888 | bytes 84412416 | tf_op jit(solution)/shard_map/dot_general | solution.py:70
  1428.0 22.4 %copy.39 = bf16[256,32768]{0,1:T(8,128)(2,1)} copy(bf16[256,32768]{1,0:T(8,128)(2,1)} %bitcast.154) | data formatting | bytes 33554432 | tf_op jit(solution)/shard_map/reshape | solution.py:160
  1450.5 25.1 %fusion.110 = bf16[256,32768]{0,1:T(8,128)(2,1)} fusion(bf16[512,32768]{0,1:T(8,128)(2,1)} %get-tuple-element.376, bf16[256,512]{1,0:T(8,128)(2,1)S(1)} %copy-done, bf16[256,32768]{0,1:T(8,128)(2,1)} %copy.39), kind=kOutput, calls=%fused_computation.198 | convolution fusion | flops 8615100416 | bytes 67371008 | tf_op jit(solution)/shard_map/dot_general | solution.py:165
  1475.6 19.8 %all-reduce = f32[512]{0:T(512)S(1)} all-reduce(f32[512]{0:T(512)S(1)} %copy-done.6), channel_id=4, replica_groups=mesh['lat'=4,'grp'=8] {'lat'}, use_global_device_ids=true, to_apply=%region_14.15.clone | all-reduce | flops 512 | bytes 4096
  1495.5 19.6 %all-reduce.2 = (f32[128]{0:T(128)S(1)}, f32[2,16,4]{1,2,0:T(4,128)S(1)}) all-reduce(f32[128]{0:T(128)S(1)} %dynamic-slice.37, f32[2,16,4]{1,2,0:T(4,128)S(1)} %copy.41), channel_id=5, replica_groups=mesh['lat'=4,'grp'=8] {'grp'}, use_global_device_ids=true, to_apply=%region_15.16.clone | all-reduce | flops 256 | bytes 2048
  1516.3 23.4 %copy.42 = bf16[256,32,1024]{2,1,0:T(8,128)(2,1)} copy(bf16[256,32,1024]{0,2,1:T(8,128)(2,1)} %bitcast.157) | data formatting | bytes 33554432
  1541.0 45.3 %reduce-scatter.11.cloned.1.call-done = f32[16,256]{1,0:T(8,128)} async-done(((f32[128,256]{1,0:T(8,128)}), f32[16,256]{1,0:T(8,128)}) %reduce-scatter.11.cloned.1.call-update) | async-done | bytes 16400 | tf_op jit(solution)/shard_map/reduce_scatter | solution.py:180
  (801 shorter events, 782.1 us)
Async XLA Ops:
  7.2 961.9 %copy-start = (bf16[256,512]{1,0:T(8,128)(2,1)S(1)}, bf16[256,512]{1,0:T(8,128)(2,1)}, u32[]{:S(2)}) copy-start(bf16[256,512]{1,0:T(8,128)(2,1)} %param.15) | copy-start | bytes 786436
  7.2 6.6 copy-start.7
  7.2 6.6 copy-start.8
  7.2 6.6 copy-start.4
  7.2 6.8 copy-start.5
  10.1 4.8 collective-permute-start
  12.5 6.6 collective-permute-start.1
  37.7 12.7 copy-start.3
  905.4 2.6 copy-start.1
  908.0 26.2 %collective-permute-start.2 = (f32[32,16,1024]{2,0,1:T(8,128)S(1)}, f32[32,16,1024]{2,0,1:T(8,128)S(1)}, u32[]{:S(2)}, u32[]{:S(2)}) collective-permute-start(f32[32,16,1024]{2,0,1:T(8,128)S(1)} %get-tuple-element.369), channel_id=1, source_target_pairs={{0,8},{8,16},{16,24},{1,9},{9,17},{17,25},{2,10},{10,18},{18,26},{... | collective-permute-start | bytes 6291464 | tf_op jit(solution)/shard_map/ppermute | solution.py:33
  922.1 12.2 collective-permute-start.3
  944.6 356.6 %all-to-all-start = ((bf16[32,256,1024]{2,0,1:T(8,128)(2,1)}), bf16[32,256,1024]{2,0,1:T(8,128)(2,1)}, u32[]{:S(2)}, u32[]{:S(2)}) async-start(bf16[32,256,1024]{2,0,1:T(8,128)(2,1)} %pad_maximum_fusion.1), calls=%async_computation | async-start | bytes 33554432 | tf_op jit(solution)/shard_map/all_to_all | solution.py:159
  950.4 500.0 %reduce-scatter.5.cloned.1.call-start = ((), (), s32[]{:S(2)}) async-start(), calls=%async_computation.5 | async-start | bytes 655360 | tf_op jit(solution)/shard_map/reduce_scatter | solution.py:173
  1316.5 11.2 copy-start.9
  1316.5 11.2 copy-start.10
  1394.3 31.1 %copy-start.12 = (u32[32]{0:T(128)S(1)}, u32[32]{0:T(128)}, u32[]{:S(2)}) copy-start(u32[32]{0:T(128)} %constant.298) | copy-start | bytes 388
  1394.3 31.7 %copy-start.11 = (u32[32]{0:T(128)S(1)}, u32[32]{0:T(128)}, u32[]{:S(2)}) copy-start(u32[32]{0:T(128)} %constant.294) | copy-start | bytes 388
  1394.3 33.6 %copy-start.2 = (f32[2,16,4]{2,0,1:T(2,128)S(1)}, f32[2,16,4]{2,0,1:T(2,128)}, u32[]{:S(2)}) copy-start(f32[2,16,4]{2,0,1:T(2,128)} %copy-done.1) | copy-start | bytes 1540
  1394.3 121.3 %reduce-scatter.9.cloned.1.call-start = ((), (), s32[]{:S(2)}) async-start(), calls=%async_computation.7 | async-start | bytes 655360 | tf_op jit(solution)/shard_map/reduce_scatter | solution.py:175
  1425.4 114.3 %reduce-scatter.7.cloned.1.call-start = ((), (), s32[]{:S(2)}) async-start(), calls=%async_computation.6 | async-start | bytes 147456 | tf_op jit(solution)/shard_map/reduce_scatter | solution.py:178
  1450.4 25.1 %copy-start.6 = (f32[512]{0:T(512)S(1)}, f32[512]{0:T(512)}, u32[]{:S(2)}) copy-start(f32[512]{0:T(512)} %get-tuple-element.375) | copy-start | bytes 6148
  1450.5 135.8 %reduce-scatter.11.cloned.1.call-start = ((), (), s32[]{:S(2)}) async-start(), calls=%async_computation.8 | async-start | bytes 147456 | tf_op jit(solution)/shard_map/reduce_scatter | solution.py:180
Sparse Core Ops, SparseCore 0:
  1394.4 33.2 reduce-scatter.4
  1430.3 28.5 reduce-scatter.8
  1462.3 60.8 reduce-scatter.6
  1526.4 59.8 reduce-scatter.10
where the time goes:
time: 1600 us; the launch traced here: 1590 us
  other arithmetic  409 us (26%)
  matrix products  393 us (25%)
  waiting for transfers between devices  354 us (22%)
  local copies, waits for them, and re-layouts  341 us (21%)
  blocking collectives  39.4 us (2%)
  starting transfers between devices  25.1 us (2%)
  loops' own time  18 us (1%)
    all_to_all x1, waiting for transfers between devices, shards(): lax.all_to_all(dy_band, 'grp', split_axis=1, concat_axis=0, tiled=True)  303 us
    add x16, other arithmetic, per_row(): current + row_sum  113 us
    dynamic_update_slice x16, local copies, waits for them, and re-layouts, per_row(): lax.dynamic_update_slice_in_dim(extended, current + row_sum, index * BH, 1)  101 us
    dot_general x64, matrix products, per_row(): product = jnp.dot(block_cot, rx_both, preferred_element_type=jnp.float32)  99 us
    dot_general x64, matrix products, per_row(): jnp.einsum('cjo,cov->cjv', ry_both, source, preferred_element_type=jnp.fl...  90 us
    reduce_sum x64, other arithmetic, per_row(): grad_rows.append(jnp.sum(lifted[:, BH:] * z_value))  84.7 us
    another operation x32, other arithmetic, per_row(): jnp.stack([jnp.stack(grad_rows), jnp.stack(grad_cols)])  80.9 us
    unnamed x32, local copies, waits for them, and re-layouts  54.5 us
  transfers between devices with their start and end apart: 9, of which 4 were waited for; matrix products, arithmetic and copies ran while one was open for 10% of the time, Pallas kernels for 0%

commit v1 on v0

--- a/solution.py
+++ b/solution.py
@@ -2,12 +2,17 @@
 
 import jax
 import jax.numpy as jnp
+import numpy as np
 from jax import lax
+from jax.experimental import pallas as pl
+from jax.experimental.pallas import tpu as pltpu
 from jax.sharding import PartitionSpec as P
 
 C = 256
 BH = 16
 BW = 256
+LANES = 128
+VMEM_BYTES = 48 * 1024 * 1024
 
 
 def extended_2(cells, sides, width):
@@ -182,7 +187,413 @@
     return (grad_inputs, summed[0] * scale, summed[1] * scale, summed[2] * scale, grad_frac)
 
 
+def taps(grid, values):
+    out = jnp.zeros(grid.shape, jnp.float32)
+    for tap in range(4):
+        out = jnp.where(grid == tap, values[tap], out)
+    return out.astype(jnp.bfloat16)
+
+
+def column_grid():
+    shape = (BW, BW + LANES)
+    return lax.broadcasted_iota(jnp.int32, shape, 1) - lax.broadcasted_iota(jnp.int32, shape, 0)
+
+
+def spread_kernel(
+    ints, floats, cot_ref, top_ref, bottom_ref, grid_ref, even_ref, odd_ref, acc, held
+):
+    step = pl.program_id(0)
+    steps = pl.num_programs(0)
+    channels, unused, columns = held.shape
+    blocks = columns // BW
+    group = grid_ref.shape[1] // BH
+
+    @pl.when(step == 0)
+    def first():
+        acc[...] = jnp.zeros_like(acc)
+        held[...] = top_ref[...]
+
+    @pl.when(step == steps - 1)
+    def last():
+        held[...] = bottom_ref[...]
+
+    @pl.when((step > 0) & (step < steps - 1))
+    def inner():
+        held[...] = cot_ref[...]
+
+    for block in range(blocks):
+        place = (step * blocks + block) * 4
+        weight = (step * blocks + block) * 16
+        row_off, row_st, col_off, col_st = [ints[place + k] for k in range(4)]
+        rx = taps(column_grid() - col_st, [floats[weight + 8 + k] for k in range(4)])
+        ry = taps(grid_ref[...] - row_st, [floats[weight + k] for k in range(4)])
+        piece = held[:, :, block * BW : (block + 1) * BW].reshape(channels * BH, BW)
+        z = jnp.dot(piece, rx, preferred_element_type=jnp.float32).astype(jnp.bfloat16)
+        rows = pl.ds(pl.multiple_of(row_off * 8, 8), 3 * BH // 2)
+        cols = pl.ds(pl.multiple_of((col_off + 2 * block) * LANES, LANES), BW + LANES)
+        for part in range(channels // group):
+            spread = jnp.dot(
+                ry,
+                z[part * group * BH : (part + 1) * group * BH],
+                preferred_element_type=jnp.float32,
+            ).reshape(group, 3 * BH // 2, BW + LANES)
+            where = (slice(part * group, (part + 1) * group), rows, cols)
+            acc[where] = acc[where] + spread
+
+    def finished():
+        left = acc[:, :BH, BW : 2 * BW] + acc[:, :BH, columns + BW :]
+        right = acc[:, :BH, columns : columns + BW] + acc[:, :BH, :BW]
+        middle = acc[:, :BH, 2 * BW : columns]
+        whole = jnp.concatenate([left, middle, right], axis=2)
+        return jnp.swapaxes(whole, 0, 1).astype(jnp.bfloat16)[None]
+
+    @pl.when((step >= 2) & (step % 2 == 0))
+    def even():
+        even_ref[...] = finished()
+
+    @pl.when((step >= 2) & (step % 2 == 1))
+    def odd():
+        odd_ref[...] = finished()
+
+    acc[:, :BH] = acc[:, BH : 2 * BH]
+    acc[:, BH : 2 * BH] = acc[:, 2 * BH :]
+    acc[:, 2 * BH :] = jnp.zeros((channels, BH, acc.shape[2]), jnp.float32)
+
+
+def spread_call(ints, floats, cotangent, top, bottom, half, halves):
+    channels, band_rows, columns = cotangent.shape
+    part = channels // halves
+    row_blocks = band_rows // BH
+    group = 8
+    across = np.arange(group * 3 * BH // 2)[:, None]
+    along = np.arange(group * BH)[None, :]
+    same = across // (3 * BH // 2) == along // BH
+    grid = np.where(same, across % (3 * BH // 2) - along % BH, -1000).astype(np.int32)
+    halo = pl.BlockSpec((part, BH, columns), lambda i, *s: (half, 0, 0))
+    result = jax.ShapeDtypeStruct((row_blocks // 2, BH, part, columns), jnp.bfloat16)
+    out_spec = pl.BlockSpec(
+        (1, BH, part, columns), lambda i, *s: (jnp.maximum(i - 2, 0) // 2, 0, 0, 0)
+    )
+    flops = 2 * (row_blocks + 2) * (columns // BW) * part * BH * (BW + LANES) * (BW + 8 * 24)
+    return pl.pallas_call(
+        spread_kernel,
+        grid_spec=pltpu.PrefetchScalarGridSpec(
+            num_scalar_prefetch=2,
+            grid=(row_blocks + 2,),
+            in_specs=[
+                pl.BlockSpec(
+                    (part, BH, columns),
+                    lambda i, *s: (half, jnp.clip(i - 1, 0, row_blocks - 1), 0),
+                ),
+                halo,
+                halo,
+                pl.BlockSpec(grid.shape, lambda i, *s: (0, 0)),
+            ],
+            out_specs=[out_spec, out_spec],
+            scratch_shapes=[
+                pltpu.VMEM((part, 3 * BH, columns + 2 * BW), jnp.float32),
+                pltpu.VMEM((part, BH, columns), jnp.bfloat16),
+            ],
+        ),
+        out_shape=[result, result],
+        compiler_params=pltpu.CompilerParams(vmem_limit_bytes=VMEM_BYTES),
+        cost_estimate=pl.CostEstimate(
+            flops=flops, bytes_accessed=4 * part * band_rows * columns, transcendentals=0
+        ),
+        name="spread",
+    )(ints, floats, cotangent, top, bottom, jnp.asarray(grid))
+
+
+def frac_kernel(
+    ints, floats, cot_ref, before_ref, here_ref, after_ref, top_ref, bottom_ref, grid_ref,
+    out_ref, window, rx_both, ry_both
+):
+    step = pl.program_id(0)
+    steps = pl.num_programs(0)
+    channels, unused, columns = cot_ref.shape
+    blocks = columns // BW
+    group = grid_ref.shape[0] // BH
+
+    def fill(rows, ref):
+        window[:, rows, BW : columns + BW] = ref[...]
+        window[:, rows, :BW] = ref[:, :, columns - BW :]
+        window[:, rows, columns + BW :] = ref[:, :, :BW]
+
+    @pl.when(step == 0)
+    def first():
+        fill(slice(0, BH), top_ref)
+
+    @pl.when(step > 0)
+    def before():
+        fill(slice(0, BH), before_ref)
+
+    fill(slice(BH, 2 * BH), here_ref)
+
+    @pl.when(step == steps - 1)
+    def last():
+        fill(slice(2 * BH, 3 * BH), bottom_ref)
+
+    @pl.when(step < steps - 1)
+    def after():
+        fill(slice(2 * BH, 3 * BH), after_ref)
+
+    @pl.when(pl.program_id(1) == 0)
+    def matrices():
+        out_ref[...] = jnp.zeros_like(out_ref)
+        for block in range(blocks):
+            place = ((step + 1) * blocks + block) * 4
+            weight = ((step + 1) * blocks + block) * 16
+            row_off, row_st, unused_off, col_st = [ints[place + k] for k in range(4)]
+            row_grid = grid_ref[...] - (row_off * 8 + row_st)
+            ry_both[block, : group * BH] = taps(row_grid, [floats[weight + k] for k in range(4)])
+            ry_both[block, group * BH :] = taps(
+                row_grid, [floats[weight + 4 + k] for k in range(4)]
+            )
+            col_grid = column_grid() - col_st
+            rx_both[block, :, : BW + LANES] = taps(
+                col_grid, [floats[weight + 8 + k] for k in range(4)]
+            )
+            rx_both[block, :, BW + LANES :] = taps(
+                col_grid, [floats[weight + 12 + k] for k in range(4)]
+            )
+
+    for block in range(blocks):
+        col_off = ints[((step + 1) * blocks + block) * 4 + 2]
+        cols = pl.ds(pl.multiple_of((col_off + 2 * block) * LANES, LANES), BW + LANES)
+        piece = cot_ref[:, :, block * BW : (block + 1) * BW].reshape(channels * BH, BW)
+        z = jnp.dot(piece, rx_both[block], preferred_element_type=jnp.float32)
+        row_total = jnp.zeros((1, BW + LANES), jnp.float32)
+        col_total = jnp.zeros((1, BW + LANES), jnp.float32)
+        for part in range(channels // group):
+            source = window[part * group : (part + 1) * group, :, cols]
+            source = source.reshape(group * 3 * BH, BW + LANES)
+            lifted = jnp.dot(ry_both[block], source, preferred_element_type=jnp.float32)
+            zs = z[part * group * BH : (part + 1) * group * BH]
+            row_total += jnp.sum(
+                lifted[group * BH :] * zs[:, : BW + LANES], axis=0, keepdims=True
+            )
+            col_total += jnp.sum(
+                lifted[: group * BH] * zs[:, BW + LANES :], axis=0, keepdims=True
+            )
+        out_ref[0, block : block + 1] += row_total
+        out_ref[0, blocks + block : blocks + block + 1] += col_total
+
+
+def frac_call(ints, floats, cotangent, advected, top, bottom):
+    channels, band_rows, columns = cotangent.shape
+    part = 16
+    row_blocks = band_rows // BH
+    blocks = columns // BW
+    group = 8
+    across = np.arange(group * BH)[:, None]
+    along = np.arange(group * 3 * BH)[None, :]
+    same = across // BH == along // (3 * BH)
+    grid = np.where(same, along % (3 * BH) - across % BH, -1000).astype(np.int32)
+
+    def rows(shift):
+        return pl.BlockSpec(
+            (part, BH, columns),
+            lambda i, c, *s: (c, jnp.clip(i + shift, 0, row_blocks - 1), 0),
+        )
+
+    halo = pl.BlockSpec((part, BH, columns), lambda i, c, *s: (c, 0, 0))
+    flops = 2 * row_blocks * blocks * channels * BH * (BW + LANES) * (2 * BW + 2 * group * 3 * BH)
+    return pl.pallas_call(
+        frac_kernel,
+        grid_spec=pltpu.PrefetchScalarGridSpec(
+            num_scalar_prefetch=2,
+            grid=(row_blocks, channels // part),
+            in_specs=[
+                rows(0),
+                rows(-1),
+                rows(0),
+                rows(1),
+                halo,
+                halo,
+                pl.BlockSpec(grid.shape, lambda i, c, *s: (0, 0)),
+            ],
+            out_specs=pl.BlockSpec((1, 2 * blocks, BW + LANES), lambda i, c, *s: (i, 0, 0)),
+            scratch_shapes=[
+                pltpu.VMEM((part, 3 * BH, columns + 2 * BW), jnp.bfloat16),
+                pltpu.VMEM((blocks, BW, 2 * (BW + LANES)), jnp.bfloat16),
+                pltpu.VMEM((blocks, 2 * group * BH, group * 3 * BH), jnp.bfloat16),
+            ],
+        ),
+        out_shape=jax.ShapeDtypeStruct((row_blocks, 2 * blocks, BW + LANES), jnp.float32),
+        compiler_params=pltpu.CompilerParams(vmem_limit_bytes=VMEM_BYTES),
+        cost_estimate=pl.CostEstimate(
+            flops=flops, bytes_accessed=8 * channels * band_rows * columns, transcendentals=0
+        ),
+        name="frac",
+    )(ints, floats, cotangent, advected, advected, advected, top, bottom, jnp.asarray(grid))
+
+
+def mlp_kernel(*refs):
+    x_ref, dy0_ref, dy1_ref, w_in_ref, w_in_t_ref, bias_ref, w_out_ref = refs[:7]
+    dx_ref, first_ref, shift_ref, second_ref, x_flat, dy_flat, dx_rows = refs[-7:]
+    width = x_ref.shape[2]
+
+    @pl.when(pl.program_id(0) == 0)
+    def clear():
+        first_ref[...] = jnp.zeros_like(first_ref)
+        shift_ref[...] = jnp.zeros_like(shift_ref)
+        second_ref[...] = jnp.zeros_like(second_ref)
+
+    x_rows = jnp.swapaxes(x_ref[...].astype(jnp.float32), 0, 1).astype(jnp.bfloat16)
+    for row in range(BH):
+        cols = slice(row * width, (row + 1) * width)
+        x_flat[:, cols] = x_rows[row]
+        dy_flat[:, 0, :, cols] = dy0_ref[:, row]
+        dy_flat[:, 1, :, cols] = dy1_ref[:, row]
+    tile = 1024
+    for start in range(0, BH * width, tile):
+        cols = slice(start, start + tile)
+        x = x_flat[:, cols]
+        dy = dy_flat[:, :, :, cols].reshape(x.shape)
+        pre = jnp.dot(w_in_t_ref[...], x, preferred_element_type=jnp.float32) + bias_ref[...]
+        sigma = jax.nn.sigmoid(pre)
+        act = (pre * sigma).astype(jnp.bfloat16)
+        dact = jnp.dot(w_out_ref[...], dy, preferred_element_type=jnp.float32)
+        dpre_wide = dact * sigma * (1.0 + pre * (1.0 - sigma))
+        dpre = dpre_wide.astype(jnp.bfloat16)
+        dx = dy.astype(jnp.float32) + jnp.dot(
+            w_in_ref[...], dpre, preferred_element_type=jnp.float32
+        )
+        for part in range(tile // width):
+            dx_rows[start // width + part] = dx[:, part * width : (part + 1) * width]
+        first_ref[...] += contract_points(x, dpre)
+        second_ref[...] += contract_points(act, dy)
+        shift_ref[...] += jnp.sum(dpre.astype(jnp.float32), axis=1, keepdims=True)
+    dx_ref[...] = jnp.swapaxes(dx_rows[...], 0, 1).astype(jnp.bfloat16)
+
+
+def mlp_call(inputs, dy0, dy1, w_in, bias_in, w_out, half, earlier):
+    channels, point_rows, columns = inputs.shape
+    hidden = w_in.shape[1]
+    sources, unused, part, unused_columns = dy0.shape
+    width = LANES
+    whole = lambda shape: pl.BlockSpec(shape, lambda j: (0, 0))
+    points = pl.BlockSpec((channels, BH, width), lambda j: (0, half, j))
+    dy_spec = pl.BlockSpec((sources, BH, part, width), lambda j: (0, 0, 0, j))
+    operands = [inputs, dy0, dy1, w_in, w_in.T, bias_in[:, None], w_out]
+    in_specs = [
+        points,
+        dy_spec,
+        dy_spec,
+        whole((channels, hidden)),
+        whole((hidden, channels)),
+        whole((hidden, 1)),
+        whole((hidden, channels)),
+    ]
+    aliases = {}
+    if earlier is not None:
+        operands.append(earlier)
+        in_specs.append(pl.BlockSpec(memory_space=pl.ANY))
+        aliases = {7: 0}
+    return pl.pallas_call(
+        mlp_kernel,
+        grid=(columns // width,),
+        in_specs=in_specs,
+        out_specs=[
+            points,
+            whole((channels, hidden)),
+            whole((hidden, 1)),
+            whole((hidden, channels)),
+        ],
+        out_shape=[
+            jax.ShapeDtypeStruct(inputs.shape, jnp.bfloat16),
+            jax.ShapeDtypeStruct((channels, hidden), jnp.float32),
+            jax.ShapeDtypeStruct((hidden, 1), jnp.float32),
+            jax.ShapeDtypeStruct((hidden, channels), jnp.float32),
+        ],
+        scratch_shapes=[
+            pltpu.VMEM((channels, BH * width), jnp.bfloat16),
+            pltpu.VMEM((sources, 2, part, BH * width), jnp.bfloat16),
+            pltpu.VMEM((BH, channels, width), jnp.float32),
+        ],
+        input_output_aliases=aliases,
+        compiler_params=pltpu.CompilerParams(vmem_limit_bytes=VMEM_BYTES),
+        cost_estimate=pl.CostEstimate(
+            flops=10 * channels * hidden * BH * columns,
+            bytes_accessed=6 * channels * BH * columns,
+            transcendentals=2 * hidden * BH * columns,
+        ),
+        name="mlp",
+    )(*operands)
+
+
+def scattered(grid, axis):
+    count = lax.axis_size(axis)
+    parts = grid.reshape((count, grid.shape[0] // count) + grid.shape[1:])
+    return jnp.sum(lax.all_to_all(parts, axis, split_axis=0, concat_axis=0, tiled=True), axis=0)
+
+
+def neighbours(cells, axis, dim, width):
+    count = lax.axis_size(axis)
+    ends = count - 1
+    head = lax.slice_in_dim(cells, 0, width, axis=dim)
+    tail = lax.slice_in_dim(cells, cells.shape[dim] - width, cells.shape[dim], axis=dim)
+    return (
+        lax.ppermute(tail, axis, [(i, i + 1) for i in range(ends)]),
+        lax.ppermute(head, axis, [(i + 1, i) for i in range(ends)]),
+    )
+
+
+def fast_shards(
+    inputs, w_in, bias_in, w_out, advected, cotangent, offsets, stencil_row, stencil_col, fracs
+):
+    band_rows, columns = advected.shape[1:]
+    hidden = w_in.shape[1]
+    blocks = columns // BW
+    row_blocks = band_rows // BH
+    places = jnp.stack([offsets[0], stencil_row, offsets[1], stencil_col], axis=-1)
+    table = jnp.concatenate([places.astype(jnp.float32), jnp.moveaxis(fracs, 0, -1)], axis=-1)
+    above, below = neighbours(table, "lat", 0, 1)
+    table = jnp.concatenate([above, table, below], axis=0)
+    ints = table[..., :4].astype(jnp.int32).reshape(-1)
+    row_w, row_s = catmull(table[..., 4])
+    col_w, col_s = catmull(table[..., 5])
+    floats = jnp.stack([*row_w, *row_s, *col_w, *col_s], axis=-1).reshape(-1)
+
+    cot_top, cot_bottom = neighbours(cotangent, "lat", 1, BH)
+
+    def to_points(cells):
+        return lax.all_to_all(cells, "grp", split_axis=0, concat_axis=0, tiled=True)
+
+    even0, odd0 = spread_call(ints, floats, cotangent, cot_top, cot_bottom, 0, 2)
+    dy_even0 = to_points(even0)
+    even1, odd1 = spread_call(ints, floats, cotangent, cot_top, cot_bottom, 1, 2)
+    dy_even1 = to_points(even1)
+    odd0, dy_even0 = lax.optimization_barrier((odd0, dy_even0))
+    dy_odd0 = to_points(odd0)
+    odd1, dy_even1 = lax.optimization_barrier((odd1, dy_even1))
+    dy_odd1 = to_points(odd1)
+
+    adv_top, adv_bottom = neighbours(advected, "lat", 1, BH)
+    frac_parts = frac_call(ints, floats, cotangent, advected, adv_top, adv_bottom)
+    frac_local = jnp.sum(frac_parts, axis=2).reshape(row_blocks, 2, blocks)
+    frac_total = lax.psum(jnp.moveaxis(frac_local, 1, 0), "grp")
+    grad_frac = frac_total / math.sqrt(C * BH * BW)
+
+    early = mlp_call(inputs, dy_even0, dy_even1, w_in, bias_in, w_out, 0, None)
+    late = mlp_call(inputs, dy_odd0, dy_odd1, w_in, bias_in, w_out, 1, early[0])
+    first, shift, second = [early[k] + late[k] for k in (1, 2, 3)]
+    merged = jnp.concatenate([first.T, second, jnp.broadcast_to(shift, (hidden, LANES))], axis=1)
+    share = scattered(scattered(merged, "lat"), "grp")
+    total_points = band_rows * columns * lax.axis_size("lat")
+    share = share * (1.0 / math.sqrt(total_points))
+    return (late[0], share[:, :C].T, share[:, 2 * C], share[:, C : 2 * C], grad_frac)
+
+
 def solution(mesh):
+    grp = mesh.shape["grp"]
+
+    def chosen(*args):
+        band_rows = args[4].shape[1]
+        channels = args[4].shape[0]
+        paired = args[0].shape[1] == 2 * BH and band_rows == 2 * BH * grp
+        return (fast_shards if paired and channels % 32 == 0 else shards)(*args)
+
     placed = (
         P(None, ("lat", "grp"), None),
         P(),
@@ -196,7 +607,7 @@
         P(None, "lat", None),
     )
     return jax.shard_map(
-        shards,
+        chosen,
         mesh=mesh,
         in_specs=placed,
         out_specs=(

time: 1600 us -> 629 us (0.39)
  other arithmetic: 409 us -> 4.95 us
  matrix products: 393 us -> 0 us
  local copies, waits for them, and re-layouts: 341 us -> 10.1 us
  Pallas kernels: 0 us -> 244 us
  waiting for transfers between devices: 354 us -> 281 us
  starting transfers between devices: 25.1 us -> 44.4 us
  loops' own time: 18 us -> 0 us
    dot_general x197 -> x0, matrix products: 393 us -> none  [the longest x64 99 us: per_row(): product = jnp.dot(block_cot, rx_both, preferred_element_type=jnp.float32)]
    pallas_call x0 -> x5, Pallas kernels: none -> 244 us  [the longest x1 84.4 us: frac_call(): pl.pallas_call(frac_kernel, grid_spec=pltpu.PrefetchScalarGridSpec(num_sc...]
    add x33 -> x2, other arithmetic: 150 us -> 0.22 us  [fast_shards(): first, shift, second = [early[k] + late[k] for k in (1, 2, 3)]]
    dynamic_update_slice x16 -> x0, local copies, waits for them, and re-layouts: 101 us -> none  [per_row(): lax.dynamic_update_slice_in_dim(extended, current + row_sum, index * BH, 1)]
    another operation x49 -> x1, other arithmetic: 95.6 us -> 0.01 us  [fast_shards(): floats = jnp.stack([*row_w, *row_s, *col_w, *col_s], axis=-1).reshape(-1)]
    reduce_sum x64 -> x3, other arithmetic: 84.7 us -> 0.92 us  [the longest x2 0.83 us: scattered(): jnp.sum(lax.all_to_all(parts, axis, split_axis=0, concat_axis=0, tiled=Tr...]
    slice x51 -> x4, local copies, waits for them, and re-layouts: 74.8 us -> 7.25 us  [the longest x2 6.02 us: neighbours(): head = lax.slice_in_dim(cells, 0, width, axis=dim)]
    unnamed x32 -> x13, local copies, waits for them, and re-layouts: 54.5 us -> 0.17 us
  transfers between devices with their start and end apart: 9 -> 11, of which waited for: 4 -> 5; matrix products, arithmetic and copies ran while one was open for 10% -> 2% of each run, Pallas kernels for 0% -> 33%
where the time goes in v1:
time: 629 us; the launch traced here: 628 us
  waiting for transfers between devices  281 us (45%)
  Pallas kernels  244 us (39%)
  starting transfers between devices  44.4 us (7%)
  blocking collectives  41.5 us (7%)
  local copies, waits for them, and re-layouts  10.1 us (2%)
    all_to_all x4, waiting for transfers between devices, to_points(): return lax.all_to_all(cells, 'grp', split_axis=0, concat_axis=0, tiled=True)  280 us
    pallas_call x1, Pallas kernels, frac_call(): pl.pallas_call(frac_kernel, grid_spec=pltpu.PrefetchScalarGridSpec(num_sc...  84.4 us
    pallas_call x2, Pallas kernels, mlp_call(): pl.pallas_call(mlp_kernel, grid=(columns // width,), in_specs=in_specs, o...  82.7 us
    pallas_call x2, Pallas kernels, spread_call(): pl.pallas_call(spread_kernel, grid_spec=pltpu.PrefetchScalarGridSpec(num_...  77.1 us
    all_to_all x4, starting transfers between devices, to_points(): return lax.all_to_all(cells, 'grp', split_axis=0, concat_axis=0, tiled=True)  24.7 us
    psum x1, blocking collectives, fast_shards(): frac_total = lax.psum(jnp.moveaxis(frac_local, 1, 0), 'grp')  21.8 us
    all_to_all x1, blocking collectives, scattered(): lax.all_to_all(parts, axis, split_axis=0, concat_axis=0, tiled=True)  19.7 us
  transfers between devices with their start and end apart: 11, of which 5 were waited for; matrix products, arithmetic and copies ran while one was open for 2% of the time, Pallas kernels for 33%

profile of v1, /device:TPU:0, one launch (start us, length us, event | category | flops | bytes accessed | tf_op | source)
XLA Modules:
  0.0 627.5 jit_solution(15624027479550313541)
XLA Ops:
  0.7 0.7 slice_bitcast_fusion.2
  1.4 0.7 add_convert_fusion
  2.1 0.8 slice_maximum_fusion
  2.9 2.3 collective-permute-start
  5.3 1.3 collective-permute-start.1
  6.6 2.8 fusion.1
  9.3 1.3 collective-permute-start.3
  10.6 5.9 collective-permute-start.2
  17.4 1.3 collective-permute-done.2.top_ref
  18.7 38.6 %spread.3 = (bf16[8,16,16,1024]{3,2,1,0:T(8,128)(2,1)}, bf16[8,16,16,1024]{3,2,1,0:T(8,128)(2,1)}) custom-call(s32[288]{0:T(512)S(1)} %reshape.25.ints, f32[1152]{0:T(1024)S(1)} %reshape.26.floats, bf16[32,256,1024]{2,1,0:T(8,128)(2,1)} %cot_ref.5, bf16[32,16,1024]{2,1,0:T(8,128)(2,1)S(1)} %collective-permute-done.2.top_ref, ...), custom_call_target="tpu_custom_call" | custom-call | flops 6341787648 | bytes 16777216 | tf_op jit(solution)/shard_map/spread/pallas_call | solution.py:278
  57.3 5.8 all-to-all-start.2
  63.1 38.5 %spread.2 = (bf16[8,16,16,1024]{3,2,1,0:T(8,128)(2,1)}, bf16[8,16,16,1024]{3,2,1,0:T(8,128)(2,1)}) custom-call(s32[288]{0:T(512)S(1)} %reshape.25.ints, f32[1152]{0:T(1024)S(1)} %reshape.26.floats, bf16[32,256,1024]{2,1,0:T(8,128)(2,1)} %cot_ref.5, bf16[32,16,1024]{2,1,0:T(8,128)(2,1)S(1)} %collective-permute-done.2.top_ref, ...), custom_call_target="tpu_custom_call" | custom-call | flops 6341787648 | bytes 16777216 | tf_op jit(solution)/shard_map/spread/pallas_call | solution.py:278
  101.6 50.0 %all-to-all-done.2.refs_2_ = bf16[8,16,16,1024]{3,2,1,0:T(8,128)(2,1)} async-done(((bf16[8,16,16,1024]{3,2,1,0:T(8,128)(2,1)}), bf16[8,16,16,1024]{3,2,1,0:T(8,128)(2,1)}, u32[]{:S(2)}, u32[]{:S(2)}) %all-to-all-start.2) | async-done | bytes 4194336 | tf_op jit(solution)/shard_map/all_to_all | solution.py:561
  151.6 9.7 %all-to-all-start = ((bf16[8,16,16,1024]{3,2,1,0:T(8,128)(2,1)}), bf16[8,16,16,1024]{3,2,1,0:T(8,128)(2,1)}, u32[]{:S(2)}, u32[]{:S(2)}) async-start(bf16[8,16,16,1024]{3,2,1,0:T(8,128)(2,1)} %get-tuple-element.22), calls=%async_computation | async-start | bytes 8388608 | tf_op jit(solution)/shard_map/all_to_all | solution.py:561
  161.3 94.8 %all-to-all-done.refs_1_ = bf16[8,16,16,1024]{3,2,1,0:T(8,128)(2,1)} async-done(((bf16[8,16,16,1024]{3,2,1,0:T(8,128)(2,1)}), bf16[8,16,16,1024]{3,2,1,0:T(8,128)(2,1)}, u32[]{:S(2)}, u32[]{:S(2)}) %all-to-all-start) | async-done | bytes 4194336 | tf_op jit(solution)/shard_map/all_to_all | solution.py:561
  256.2 4.6 all-to-all-start.3
  260.8 93.7 %all-to-all-done.3.refs_2_ = bf16[8,16,16,1024]{3,2,1,0:T(8,128)(2,1)} async-done(((bf16[8,16,16,1024]{3,2,1,0:T(8,128)(2,1)}), bf16[8,16,16,1024]{3,2,1,0:T(8,128)(2,1)}, u32[]{:S(2)}, u32[]{:S(2)}) %all-to-all-start.3) | async-done | bytes 4194336 | tf_op jit(solution)/shard_map/all_to_all | solution.py:561
  354.5 4.6 all-to-all-start.1
  359.1 3.3 fusion
  362.4 1.3 collective-permute-start.5
  363.7 4.0 collective-permute-start.4
  368.0 41.4 %mlp.2 = (bf16[256,32,1024]{2,1,0:T(8,128)(2,1)}, f32[256,512]{1,0:T(8,128)S(1)}, f32[512,1]{1,0:T(8,128)S(1)}, f32[512,256]{1,0:T(8,128)S(1)}) custom-call(bf16[256,32,1024]{2,1,0:T(8,128)(2,1)} %refs_0_.3, bf16[8,16,16,1024]{3,2,1,0:T(8,128)(2,1)} %all-to-all-done.refs_1_, bf16[8,16,16,1024]{3,2,1,0:T(8,128)(2,1)} %all-to-all-done.2.refs_2_, ...), custom_call_target="tpu_custom_call" | custom-call | flops 21474836480 | bytes 25165824 | tf_op jit(solution)/shard_map/mlp/pallas_call | solution.py:493
  409.4 1.0 copy.42
  410.4 41.6 %all-to-all-done.1.refs_1_ = bf16[8,16,16,1024]{3,2,1,0:T(8,128)(2,1)} async-done(((bf16[8,16,16,1024]{3,2,1,0:T(8,128)(2,1)}), bf16[8,16,16,1024]{3,2,1,0:T(8,128)(2,1)}, u32[]{:S(2)}, u32[]{:S(2)}) %all-to-all-start.1) | async-done | bytes 4194336 | tf_op jit(solution)/shard_map/all_to_all | solution.py:561
  452.0 41.4 %mlp.3 = (bf16[256,32,1024]{2,1,0:T(8,128)(2,1)}, f32[256,512]{1,0:T(8,128)S(1)}, f32[512,1]{1,0:T(8,128)S(1)}, f32[512,256]{1,0:T(8,128)S(1)}) custom-call(bf16[256,32,1024]{2,1,0:T(8,128)(2,1)} %refs_0_.3, bf16[8,16,16,1024]{3,2,1,0:T(8,128)(2,1)} %all-to-all-done.1.refs_1_, ...), custom_call_target="tpu_custom_call", output_to_operand_aliasing={{0}: (7, {})} | custom-call | flops 21474836480 | bytes 25165824 | tf_op jit(solution)/shard_map/mlp/pallas_call | solution.py:493
  493.8 1.1 add_bitcast_fusion
  495.1 19.7 %all_to_all.30 = f32[4,128,640]{2,1,0:T(8,128)S(1)} all-to-all(f32[4,128,640]{2,1,0:T(8,128)S(1)} %bitcast.20), channel_id=1, replica_groups=mesh['lat'=4,'grp'=8] {'lat'}, dimensions={0} | all-to-all | bytes 2621440 | tf_op jit(solution)/shard_map/all_to_all | solution.py:528
  514.8 0.8 reduce_sum.27
  515.7 3.7 all-to-all-start.5
  519.3 84.4 %frac.1 = f32[16,8,384]{2,1,0:T(8,128)S(1)} custom-call(s32[288]{0:T(512)S(1)} %reshape.25.ints, f32[1152]{0:T(1024)S(1)} %reshape.26.floats, bf16[32,256,1024]{2,1,0:T(8,128)(2,1)} %cot_ref.5, bf16[32,256,1024]{2,1,0:T(8,128)(2,1)} %after_ref.1, bf16[32,256,1024]{2,1,0:T(8,128)(2,1)} %after_ref.1, bf16[32,256,1024]{2,1,0:T(8,128)(2,1)} %after_ref.1, ...), custom_call_target="tpu_custom_call" | custom-call | flops 32212254720 | bytes 67108864 | tf_op jit(solution)/shard_map/frac/pallas_call | solution.py:401
  603.9 21.8 %psum.7 = f32[2,16,4]{1,2,0:T(4,128)S(1)} all-reduce(f32[2,16,4]{1,2,0:T(4,128)S(1)} %bitcast.25), channel_id=1, replica_groups=mesh['lat'=4,'grp'=8] {'grp'}, use_global_device_ids=true, to_apply=%region_3.0 | all-reduce | flops 128 | bytes 1024 | tf_op jit(solution)/shard_map/psum | solution.py:575
  626.3 0.6 slice_reduce_fusion
  (53 shorter events, 3.2 us)
Async XLA Ops:
  0.6 18.1 %copy-start.3 = (s32[192,128]{1,0:T(8,128)S(1)}, s32[192,128]{1,0:T(8,128)}, u32[]{:S(2)}) copy-start(s32[192,128]{1,0:T(8,128)} %constant.35.clone.grid_ref) | copy-start | bytes 294916
  0.6 15.9 %copy-start.4 = (f32[2,16,4]{1,2,0:T(4,128)S(1)}, f32[2,16,4]{1,2,0:T(4,128)}, u32[]{:S(2)}) copy-start(f32[2,16,4]{1,2,0:T(4,128)} %param.22) | copy-start | bytes 1540
  2.9 13.6 %collective-permute-start = (f32[1,4,6]{0,1,2:T(4,128)S(1)}, f32[1,4,6]{0,1,2:T(4,128)S(1)}, u32[]{:S(2)}, u32[]{:S(2)}) collective-permute-start(f32[1,4,6]{0,1,2:T(4,128)S(1)} %get-tuple-element.47), channel_id=1, source_target_pairs={{0,8},{8,16},{16,24},{1,9},{9,17},{17,25},{2,10},{10,18},{18,26},{... | collective-permute-start | bytes 296 | tf_op jit(solution)/shard_map/ppermute | solution.py:537
  5.3 11.2 %collective-permute-start.1 = (f32[1,4,6]{0,1,2:T(4,128)S(1)}, f32[1,4,6]{0,1,2:T(4,128)S(1)}, u32[]{:S(2)}, u32[]{:S(2)}) collective-permute-start(f32[1,4,6]{0,1,2:T(4,128)S(1)} %get-tuple-element.48), channel_id=1, source_target_pairs={{8,0},{16,8},{24,16},{9,1},{17,9},{25,17},{10,2},{18,10},{26,18},{... | collective-permute-start | bytes 296 | tf_op jit(solution)/shard_map/ppermute | solution.py:538
  9.3 8.1 %collective-permute-start.3 = (bf16[32,16,1024]{2,1,0:T(8,128)(2,1)}, bf16[32,16,1024]{2,1,0:T(8,128)(2,1)S(1)}, u32[]{:S(2)}, u32[]{:S(2)}) collective-permute-start(bf16[32,16,1024]{2,1,0:T(8,128)(2,1)} %get-tuple-element.43), channel_id=1, source_target_pairs={{8,0},{16,8},{24,16},{9,1},{17,9},{25,17},{10,2},{18,10},{26,18},{... | collective-permute-start | bytes 3145736 | tf_op jit(solution)/shard_map/ppermute | solution.py:538
  10.6 8.1 %collective-permute-start.2 = (bf16[32,16,1024]{2,1,0:T(8,128)(2,1)S(1)}, bf16[32,16,1024]{2,1,0:T(8,128)(2,1)S(1)}, u32[]{:S(2)}, u32[]{:S(2)}) collective-permute-start(bf16[32,16,1024]{2,1,0:T(8,128)(2,1)S(1)} %get-tuple-element.44), channel_id=1, source_target_pairs={{0,8},{8,16},{16,24},{1,9},{9,17},{17,25},{2,10},{10,18},{18,26},{... | collective-permute-start | bytes 3145736 | tf_op jit(solution)/shard_map/ppermute | solution.py:537
  57.3 94.4 %all-to-all-start.2 = ((bf16[8,16,16,1024]{3,2,1,0:T(8,128)(2,1)}), bf16[8,16,16,1024]{3,2,1,0:T(8,128)(2,1)}, u32[]{:S(2)}, u32[]{:S(2)}) async-start(bf16[8,16,16,1024]{3,2,1,0:T(8,128)(2,1)} %get-tuple-element.25), calls=%async_computation.2 | async-start | bytes 8388608 | tf_op jit(solution)/shard_map/all_to_all | solution.py:561
  151.6 104.5 %all-to-all-start = ((bf16[8,16,16,1024]{3,2,1,0:T(8,128)(2,1)}), bf16[8,16,16,1024]{3,2,1,0:T(8,128)(2,1)}, u32[]{:S(2)}, u32[]{:S(2)}) async-start(bf16[8,16,16,1024]{3,2,1,0:T(8,128)(2,1)} %get-tuple-element.22), calls=%async_computation | async-start | bytes 8388608 | tf_op jit(solution)/shard_map/all_to_all | solution.py:561
  256.2 98.3 %all-to-all-start.3 = ((bf16[8,16,16,1024]{3,2,1,0:T(8,128)(2,1)}), bf16[8,16,16,1024]{3,2,1,0:T(8,128)(2,1)}, u32[]{:S(2)}, u32[]{:S(2)}) async-start(bf16[8,16,16,1024]{3,2,1,0:T(8,128)(2,1)} %get-tuple-element.26), calls=%async_computation.3 | async-start | bytes 8388608 | tf_op jit(solution)/shard_map/all_to_all | solution.py:561
  354.5 97.5 %all-to-all-start.1 = ((bf16[8,16,16,1024]{3,2,1,0:T(8,128)(2,1)}), bf16[8,16,16,1024]{3,2,1,0:T(8,128)(2,1)}, u32[]{:S(2)}, u32[]{:S(2)}) async-start(bf16[8,16,16,1024]{3,2,1,0:T(8,128)(2,1)} %get-tuple-element.23), calls=%async_computation.1 | async-start | bytes 8388608 | tf_op jit(solution)/shard_map/all_to_all | solution.py:561
  359.1 8.6 %copy-start.5 = (f32[512]{0:T(512)S(1)}, f32[512]{0:T(512)}, u32[]{:S(2)}) copy-start(f32[512]{0:T(512)} %param.15) | copy-start | bytes 6148
  359.1 8.8 %copy-start = (bf16[256,512]{1,0:T(8,128)(2,1)S(1)}, bf16[256,512]{1,0:T(8,128)(2,1)}, u32[]{:S(2)}) copy-start(bf16[256,512]{1,0:T(8,128)(2,1)} %refs_3_.3) | copy-start | bytes 786436
  359.1 8.9 %copy-start.1 = (bf16[512,256]{1,0:T(8,128)(2,1)S(1)}, bf16[512,256]{1,0:T(8,128)(2,1)}, u32[]{:S(2)}) copy-start(bf16[512,256]{1,0:T(8,128)(2,1)} %refs_6_.3) | copy-start | bytes 786436
  362.4 156.9 %collective-permute-start.5 = (bf16[32,16,1024]{2,1,0:T(8,128)(2,1)}, bf16[32,16,1024]{2,1,0:T(8,128)(2,1)}, u32[]{:S(2)}, u32[]{:S(2)}) collective-permute-start(bf16[32,16,1024]{2,1,0:T(8,128)(2,1)} %get-tuple-element.41), channel_id=1, source_target_pairs={{8,0},{16,8},{24,16},{9,1},{17,9},{25,17},{10,2},{18,10},{26,18},{... | collective-permute-start | bytes 3145736 | tf_op jit(solution)/shard_map/ppermute | solution.py:538
  363.7 155.7 %collective-permute-start.4 = (bf16[32,16,1024]{2,1,0:T(8,128)(2,1)}, bf16[32,16,1024]{2,1,0:T(8,128)(2,1)}, u32[]{:S(2)}, u32[]{:S(2)}) collective-permute-start(bf16[32,16,1024]{2,1,0:T(8,128)(2,1)} %get-tuple-element.42), channel_id=1, source_target_pairs={{0,8},{8,16},{16,24},{1,9},{9,17},{17,25},{2,10},{10,18},{18,26},{... | collective-permute-start | bytes 3145736 | tf_op jit(solution)/shard_map/ppermute | solution.py:537
  494.9 24.4 %copy-start.2 = (s32[128,384]{1,0:T(8,128)S(1)}, s32[128,384]{1,0:T(8,128)}, u32[]{:S(2)}) copy-start(s32[128,384]{1,0:T(8,128)} %constant.36.clone.grid_ref) | copy-start | bytes 589828
  515.7 110.6 %all-to-all-start.5 = ((f32[8,16,640]{2,1,0:T(8,128)}), f32[8,16,640]{2,1,0:T(8,128)S(1)}, u32[]{:S(2)}, u32[]{:S(2)}) async-start(f32[8,16,640]{2,1,0:T(8,128)} %bitcast.9), calls=%async_computation.5 | async-start | bytes 655360 | tf_op jit(solution)/shard_map/all_to_all | solution.py:528

commit v2 on v1

--- a/solution.py
+++ b/solution.py
@@ -194,9 +194,14 @@
     return out.astype(jnp.bfloat16)
 
 
-def column_grid():
-    shape = (BW, BW + LANES)
-    return lax.broadcasted_iota(jnp.int32, shape, 1) - lax.broadcasted_iota(jnp.int32, shape, 0)
+def column_matrix(position, values):
+    shape = (BW // 2, BW)
+    grid = lax.broadcasted_iota(jnp.int32, shape, 1) - lax.broadcasted_iota(jnp.int32, shape, 0)
+    corner = taps(grid - position, values)
+    empty = jnp.zeros((BW // 2, LANES), jnp.bfloat16)
+    upper = jnp.concatenate([corner, empty], axis=1)
+    lower = jnp.concatenate([empty, corner], axis=1)
+    return jnp.concatenate([upper, lower], axis=0)
 
 
 def spread_kernel(
@@ -225,7 +230,7 @@
         place = (step * blocks + block) * 4
         weight = (step * blocks + block) * 16
         row_off, row_st, col_off, col_st = [ints[place + k] for k in range(4)]
-        rx = taps(column_grid() - col_st, [floats[weight + 8 + k] for k in range(4)])
+        rx = column_matrix(col_st, [floats[weight + 8 + k] for k in range(4)])
         ry = taps(grid_ref[...] - row_st, [floats[weight + k] for k in range(4)])
         piece = held[:, :, block * BW : (block + 1) * BW].reshape(channels * BH, BW)
         z = jnp.dot(piece, rx, preferred_element_type=jnp.float32).astype(jnp.bfloat16)
@@ -260,16 +265,16 @@
     acc[:, 2 * BH :] = jnp.zeros((channels, BH, acc.shape[2]), jnp.float32)
 
 
-def spread_call(ints, floats, cotangent, top, bottom, half, halves):
+def spread_call(ints, floats, cotangent, top, bottom):
     channels, band_rows, columns = cotangent.shape
-    part = channels // halves
+    part = channels
     row_blocks = band_rows // BH
     group = 8
     across = np.arange(group * 3 * BH // 2)[:, None]
     along = np.arange(group * BH)[None, :]
     same = across // (3 * BH // 2) == along // BH
     grid = np.where(same, across % (3 * BH // 2) - along % BH, -1000).astype(np.int32)
-    halo = pl.BlockSpec((part, BH, columns), lambda i, *s: (half, 0, 0))
+    halo = pl.BlockSpec((part, BH, columns), lambda i, *s: (0, 0, 0))
     result = jax.ShapeDtypeStruct((row_blocks // 2, BH, part, columns), jnp.bfloat16)
     out_spec = pl.BlockSpec(
         (1, BH, part, columns), lambda i, *s: (jnp.maximum(i - 2, 0) // 2, 0, 0, 0)
@@ -283,7 +288,7 @@
             in_specs=[
                 pl.BlockSpec(
                     (part, BH, columns),
-                    lambda i, *s: (half, jnp.clip(i - 1, 0, row_blocks - 1), 0),
+                    lambda i, *s: (0, jnp.clip(i - 1, 0, row_blocks - 1), 0),
                 ),
                 halo,
                 halo,
@@ -349,12 +354,11 @@
             ry_both[block, group * BH :] = taps(
                 row_grid, [floats[weight + 4 + k] for k in range(4)]
             )
-            col_grid = column_grid() - col_st
-            rx_both[block, :, : BW + LANES] = taps(
-                col_grid, [floats[weight + 8 + k] for k in range(4)]
+            rx_both[block, :, : BW + LANES] = column_matrix(
+                col_st, [floats[weight + 8 + k] for k in range(4)]
             )
-            rx_both[block, :, BW + LANES :] = taps(
-                col_grid, [floats[weight + 12 + k] for k in range(4)]
+            rx_both[block, :, BW + LANES :] = column_matrix(
+                col_st, [floats[weight + 12 + k] for k in range(4)]
             )
 
     for block in range(blocks):
@@ -429,7 +433,7 @@
 
 
 def mlp_kernel(*refs):
-    x_ref, dy0_ref, dy1_ref, w_in_ref, w_in_t_ref, bias_ref, w_out_ref = refs[:7]
+    x_ref, dy_ref, w_in_ref, w_in_t_ref, bias_ref, w_out_ref = refs[:6]
     dx_ref, first_ref, shift_ref, second_ref, x_flat, dy_flat, dx_rows = refs[-7:]
     width = x_ref.shape[2]
 
@@ -443,13 +447,12 @@
     for row in range(BH):
         cols = slice(row * width, (row + 1) * width)
         x_flat[:, cols] = x_rows[row]
-        dy_flat[:, 0, :, cols] = dy0_ref[:, row]
-        dy_flat[:, 1, :, cols] = dy1_ref[:, row]
+        dy_flat[:, :, cols] = dy_ref[:, row]
     tile = 1024
     for start in range(0, BH * width, tile):
         cols = slice(start, start + tile)
         x = x_flat[:, cols]
-        dy = dy_flat[:, :, :, cols].reshape(x.shape)
+        dy = dy_flat[:, :, cols].reshape(x.shape)
         pre = jnp.dot(w_in_t_ref[...], x, preferred_element_type=jnp.float32) + bias_ref[...]
         sigma = jax.nn.sigmoid(pre)
         act = (pre * sigma).astype(jnp.bfloat16)
@@ -467,18 +470,17 @@
     dx_ref[...] = jnp.swapaxes(dx_rows[...], 0, 1).astype(jnp.bfloat16)
 
 
-def mlp_call(inputs, dy0, dy1, w_in, bias_in, w_out, half, earlier):
+def mlp_call(inputs, dy, w_in, bias_in, w_out, half, earlier):
     channels, point_rows, columns = inputs.shape
     hidden = w_in.shape[1]
-    sources, unused, part, unused_columns = dy0.shape
+    sources, unused, part, unused_columns = dy.shape
     width = LANES
     whole = lambda shape: pl.BlockSpec(shape, lambda j: (0, 0))
     points = pl.BlockSpec((channels, BH, width), lambda j: (0, half, j))
     dy_spec = pl.BlockSpec((sources, BH, part, width), lambda j: (0, 0, 0, j))
-    operands = [inputs, dy0, dy1, w_in, w_in.T, bias_in[:, None], w_out]
+    operands = [inputs, dy, w_in, w_in.T, bias_in[:, None], w_out]
     in_specs = [
         points,
-        dy_spec,
         dy_spec,
         whole((channels, hidden)),
         whole((hidden, channels)),
@@ -489,7 +491,7 @@
     if earlier is not None:
         operands.append(earlier)
         in_specs.append(pl.BlockSpec(memory_space=pl.ANY))
-        aliases = {7: 0}
+        aliases = {6: 0}
     return pl.pallas_call(
         mlp_kernel,
         grid=(columns // width,),
@@ -508,7 +510,7 @@
         ],
         scratch_shapes=[
             pltpu.VMEM((channels, BH * width), jnp.bfloat16),
-            pltpu.VMEM((sources, 2, part, BH * width), jnp.bfloat16),
+            pltpu.VMEM((sources, part, BH * width), jnp.bfloat16),
             pltpu.VMEM((BH, channels, width), jnp.float32),
         ],
         input_output_aliases=aliases,
@@ -522,10 +524,13 @@
     )(*operands)
 
 
-def scattered(grid, axis):
+def scattered(parts, axis):
+    return jnp.sum(lax.all_to_all(parts, axis, split_axis=0, concat_axis=0, tiled=True), axis=0)
+
+
+def parts_of(grid, axis):
     count = lax.axis_size(axis)
-    parts = grid.reshape((count, grid.shape[0] // count) + grid.shape[1:])
-    return jnp.sum(lax.all_to_all(parts, axis, split_axis=0, concat_axis=0, tiled=True), axis=0)
+    return grid.reshape((count, grid.shape[0] // count) + grid.shape[1:])
 
 
 def neighbours(cells, axis, dim, width):
@@ -560,28 +565,29 @@
     def to_points(cells):
         return lax.all_to_all(cells, "grp", split_axis=0, concat_axis=0, tiled=True)
 
-    even0, odd0 = spread_call(ints, floats, cotangent, cot_top, cot_bottom, 0, 2)
-    dy_even0 = to_points(even0)
-    even1, odd1 = spread_call(ints, floats, cotangent, cot_top, cot_bottom, 1, 2)
-    dy_even1 = to_points(even1)
-    odd0, dy_even0 = lax.optimization_barrier((odd0, dy_even0))
-    dy_odd0 = to_points(odd0)
-    odd1, dy_even1 = lax.optimization_barrier((odd1, dy_even1))
-    dy_odd1 = to_points(odd1)
-
+    even, odd = spread_call(ints, floats, cotangent, cot_top, cot_bottom)
+    dy_even = to_points(even)
     adv_top, adv_bottom = neighbours(advected, "lat", 1, BH)
     frac_parts = frac_call(ints, floats, cotangent, advected, adv_top, adv_bottom)
+    odd, dy_even, frac_parts = lax.optimization_barrier((odd, dy_even, frac_parts))
+    dy_odd = to_points(odd)
     frac_local = jnp.sum(frac_parts, axis=2).reshape(row_blocks, 2, blocks)
-    frac_total = lax.psum(jnp.moveaxis(frac_local, 1, 0), "grp")
-    grad_frac = frac_total / math.sqrt(C * BH * BW)
-
-    early = mlp_call(inputs, dy_even0, dy_even1, w_in, bias_in, w_out, 0, None)
-    late = mlp_call(inputs, dy_odd0, dy_odd1, w_in, bias_in, w_out, 1, early[0])
+    frac_local = jnp.moveaxis(frac_local, 1, 0)
+
+    early = mlp_call(inputs, dy_even, w_in, bias_in, w_out, 0, None)
+    late = mlp_call(inputs, dy_odd, w_in, bias_in, w_out, 1, early[0])
     first, shift, second = [early[k] + late[k] for k in (1, 2, 3)]
     merged = jnp.concatenate([first.T, second, jnp.broadcast_to(shift, (hidden, LANES))], axis=1)
-    share = scattered(scattered(merged, "lat"), "grp")
+    parts = parts_of(scattered(parts_of(merged, "lat"), "lat"), "grp")
+    count, depth, width = parts.shape
+    extra = -(-frac_local.size // width)
+    padded = jnp.pad(frac_local.reshape(-1), (0, extra * width - frac_local.size))
+    every = jnp.broadcast_to(padded.reshape(1, extra, width), (count, extra, width))
+    share = scattered(jnp.concatenate([parts, every], axis=1), "grp")
+    frac_total = share[depth:].reshape(-1)[: frac_local.size].reshape(frac_local.shape)
+    grad_frac = frac_total / math.sqrt(C * BH * BW)
     total_points = band_rows * columns * lax.axis_size("lat")
-    share = share * (1.0 / math.sqrt(total_points))
+    share = share[:depth] * (1.0 / math.sqrt(total_points))
     return (late[0], share[:, :C].T, share[:, 2 * C], share[:, C : 2 * C], grad_frac)
 
 

time: 629 us -> 536 us (0.85)
  waiting for transfers between devices: 281 us -> 244 us
  Pallas kernels: 244 us -> 209 us
  blocking collectives: 41.5 us -> 17 us
    all_to_all x4 -> x2, waiting for transfers between devices: 280 us -> 225 us  [to_points(): return lax.all_to_all(cells, 'grp', split_axis=0, concat_axis=0, tiled=True)]
    pallas_call x2 -> x1, Pallas kernels: 77.1 us -> 51.3 us  [spread_call(): pl.pallas_call(spread_kernel, grid_spec=pltpu.PrefetchScalarGridSpec(num_...]
    psum x1 -> x0, blocking collectives: 21.8 us -> none  [fast_shards(): frac_total = lax.psum(jnp.moveaxis(frac_local, 1, 0), 'grp')]
    all_to_all x1, waiting for transfers between devices: 0.01 us -> 16.9 us  [scattered(): lax.all_to_all(parts, axis, split_axis=0, concat_axis=0, tiled=True)]
    pallas_call x1, Pallas kernels: 84.4 us -> 74.4 us  [frac_call(): pl.pallas_call(frac_kernel, grid_spec=pltpu.PrefetchScalarGridSpec(num_sc...]
    ppermute x3, starting transfers between devices: 12.3 us -> 21 us  [neighbours(): lax.ppermute(tail, axis, [(i, i + 1) for i in range(ends)])]
    all_to_all x4 -> x2, starting transfers between devices: 24.7 us -> 18.4 us  [to_points(): return lax.all_to_all(cells, 'grp', split_axis=0, concat_axis=0, tiled=True)]
  transfers between devices with their start and end apart: 11 -> 9, of which waited for: 5 -> 5; matrix products, arithmetic and copies ran while one was open for 2% -> 2% of each run, Pallas kernels for 33% -> 22%
where the time goes in v2:
time: 536 us; the launch traced here: 535 us
  waiting for transfers between devices  244 us (46%)
  Pallas kernels  209 us (39%)
  starting transfers between devices  46.8 us (9%)
  blocking collectives  17 us (3%)
  local copies, waits for them, and re-layouts  10.5 us (2%)
  other arithmetic  6.82 us (1%)
    all_to_all x2, waiting for transfers between devices, to_points(): return lax.all_to_all(cells, 'grp', split_axis=0, concat_axis=0, tiled=True)  225 us
    pallas_call x2, Pallas kernels, mlp_call(): pl.pallas_call(mlp_kernel, grid=(columns // width,), in_specs=in_specs, o...  82.9 us
    pallas_call x1, Pallas kernels, frac_call(): pl.pallas_call(frac_kernel, grid_spec=pltpu.PrefetchScalarGridSpec(num_sc...  74.4 us
    pallas_call x1, Pallas kernels, spread_call(): pl.pallas_call(spread_kernel, grid_spec=pltpu.PrefetchScalarGridSpec(num_...  51.3 us
    ppermute x3, starting transfers between devices, neighbours(): lax.ppermute(tail, axis, [(i, i + 1) for i in range(ends)])  21 us
    all_to_all x2, starting transfers between devices, to_points(): return lax.all_to_all(cells, 'grp', split_axis=0, concat_axis=0, tiled=True)  18.4 us
    all_to_all x1, blocking collectives, scattered(): lax.all_to_all(parts, axis, split_axis=0, concat_axis=0, tiled=True)  17 us
    all_to_all x1, waiting for transfers between devices, scattered(): lax.all_to_all(parts, axis, split_axis=0, concat_axis=0, tiled=True)  16.9 us
  transfers between devices with their start and end apart: 9, of which 5 were waited for; matrix products, arithmetic and copies ran while one was open for 2% of the time, Pallas kernels for 22%

profile of v2, /device:TPU:0, one launch (start us, length us, event | category | flops | bytes accessed | tf_op | source)
XLA Modules:
  0.0 534.8 jit_solution(17244854880352955225)
XLA Ops:
  0.6 0.7 slice_bitcast_fusion.2
  1.3 0.7 add_convert_fusion
  2.0 0.8 slice_maximum_fusion
  2.9 2.3 collective-permute-start
  5.2 1.3 collective-permute-start.1
  6.5 2.8 fusion.2
  9.3 1.3 collective-permute-start.3
  10.6 5.9 %collective-permute-start.2 = (bf16[32,16,1024]{2,1,0:T(8,128)(2,1)S(1)}, bf16[32,16,1024]{2,1,0:T(8,128)(2,1)S(1)}, u32[]{:S(2)}, u32[]{:S(2)}) collective-permute-start(bf16[32,16,1024]{2,1,0:T(8,128)(2,1)S(1)} %get-tuple-element.63), channel_id=1, source_target_pairs={{0,8},{8,16},{16,24},{1,9},{9,17},{17,25},{2,10},{10,18},{18,26},{... | collective-permute-start | bytes 3145736 | tf_op jit(solution)/shard_map/ppermute | solution.py:542
  16.5 0.8 pad_maximum_fusion.3
  17.5 0.8 constant_dynamic-update-slice_fusion.15
  18.4 0.8 constant_dynamic-update-slice_fusion.7
  19.5 0.9 copy-done.3
  20.4 51.3 %spread.1 = (bf16[8,16,32,1024]{3,2,1,0:T(8,128)(2,1)}, bf16[8,16,32,1024]{3,2,1,0:T(8,128)(2,1)}) custom-call(s32[288]{0:T(512)S(1)} %reshape.38.ints, f32[1152]{0:T(1024)S(1)} %reshape.39.floats, bf16[32,256,1024]{2,1,0:T(8,128)(2,1)} %cot_ref.3, bf16[32,16,1024]{2,1,0:T(8,128)(2,1)S(1)} %collective-permute-done.2.top_ref, ...), custom_call_target="tpu_custom_call" | custom-call | flops 12683575296 | bytes 33554432 | tf_op jit(solution)/shard_map/spread/pallas_call | solution.py:283
  71.7 5.9 %all-to-all-start = ((bf16[8,16,32,1024]{3,2,1,0:T(8,128)(2,1)}), bf16[8,16,32,1024]{3,2,1,0:T(8,128)(2,1)}, u32[]{:S(2)}, u32[]{:S(2)}) async-start(bf16[8,16,32,1024]{3,2,1,0:T(8,128)(2,1)} %get-tuple-element.19), calls=%async_computation | async-start | bytes 16777216 | tf_op jit(solution)/shard_map/all_to_all | solution.py:566
  77.6 1.8 fusion.1
  79.4 1.3 collective-permute-start.5
  80.7 12.8 %collective-permute-start.4 = (bf16[32,16,1024]{2,1,0:T(8,128)(2,1)S(1)}, bf16[32,16,1024]{2,1,0:T(8,128)(2,1)S(1)}, u32[]{:S(2)}, u32[]{:S(2)}) collective-permute-start(bf16[32,16,1024]{2,1,0:T(8,128)(2,1)S(1)} %get-tuple-element.61), channel_id=1, source_target_pairs={{0,8},{8,16},{16,24},{1,9},{9,17},{17,25},{2,10},{10,18},{18,26},{... | collective-permute-start | bytes 3145736 | tf_op jit(solution)/shard_map/ppermute | solution.py:542
  93.6 2.1 collective-permute-done.4.top_ref
  95.7 74.4 %frac.1 = f32[16,8,384]{2,1,0:T(8,128)S(1)} custom-call(s32[288]{0:T(512)S(1)} %reshape.38.ints, f32[1152]{0:T(1024)S(1)} %reshape.39.floats, bf16[32,256,1024]{2,1,0:T(8,128)(2,1)} %cot_ref.3, bf16[32,256,1024]{2,1,0:T(8,128)(2,1)} %after_ref.1, bf16[32,256,1024]{2,1,0:T(8,128)(2,1)} %after_ref.1, bf16[32,256,1024]{2,1,0:T(8,128)(2,1)} %after_ref.1, ...), custom_call_target="tpu_custom_call" | custom-call | flops 32212254720 | bytes 67108864 | tf_op jit(solution)/shard_map/frac/pallas_call | solution.py:405
  170.0 83.3 %all-to-all-done.refs_1_ = bf16[8,16,32,1024]{3,2,1,0:T(8,128)(2,1)} async-done(((bf16[8,16,32,1024]{3,2,1,0:T(8,128)(2,1)}), bf16[8,16,32,1024]{3,2,1,0:T(8,128)(2,1)}, u32[]{:S(2)}, u32[]{:S(2)}) %all-to-all-start) | async-done | bytes 8388640 | tf_op jit(solution)/shard_map/all_to_all | solution.py:566
  253.4 12.5 %all-to-all-start.1 = ((bf16[8,16,32,1024]{3,2,1,0:T(8,128)(2,1)}), bf16[8,16,32,1024]{3,2,1,0:T(8,128)(2,1)}, u32[]{:S(2)}, u32[]{:S(2)}) async-start(bf16[8,16,32,1024]{3,2,1,0:T(8,128)(2,1)} %get-tuple-element.20), calls=%async_computation.1 | async-start | bytes 16777216 | tf_op jit(solution)/shard_map/all_to_all | solution.py:566
  266.2 41.4 %mlp.2 = (bf16[256,32,1024]{2,1,0:T(8,128)(2,1)}, f32[256,512]{1,0:T(8,128)S(1)}, f32[512,1]{1,0:T(8,128)S(1)}, f32[512,256]{1,0:T(8,128)S(1)}) custom-call(bf16[256,32,1024]{2,1,0:T(8,128)(2,1)} %refs_0_.3, bf16[8,16,32,1024]{3,2,1,0:T(8,128)(2,1)} %all-to-all-done.refs_1_, bf16[256,512]{1,0:T(8,128)(2,1)S(1)} %copy-done, bf16[512,256]{1,0:T(8,128)(2,1)S(1)} %bitcast.18, ...), custom_call_target="tpu_custom_call" | custom-call | flops 21474836480 | bytes 25165824 | tf_op jit(solution)/shard_map/mlp/pallas_call | solution.py:495
  307.6 1.0 copy.57
  308.6 141.8 %all-to-all-done.1.refs_1_ = bf16[8,16,32,1024]{3,2,1,0:T(8,128)(2,1)} async-done(((bf16[8,16,32,1024]{3,2,1,0:T(8,128)(2,1)}), bf16[8,16,32,1024]{3,2,1,0:T(8,128)(2,1)}, u32[]{:S(2)}, u32[]{:S(2)}) %all-to-all-start.1) | async-done | bytes 8388640 | tf_op jit(solution)/shard_map/all_to_all | solution.py:566
  450.5 41.4 %mlp.3 = (bf16[256,32,1024]{2,1,0:T(8,128)(2,1)}, f32[256,512]{1,0:T(8,128)S(1)}, f32[512,1]{1,0:T(8,128)S(1)}, f32[512,256]{1,0:T(8,128)S(1)}) custom-call(bf16[256,32,1024]{2,1,0:T(8,128)(2,1)} %refs_0_.3, bf16[8,16,32,1024]{3,2,1,0:T(8,128)(2,1)} %all-to-all-done.1.refs_1_, bf16[256,512]{1,0:T(8,128)(2,1)S(1)} %copy-done, ...), custom_call_target="tpu_custom_call", output_to_operand_aliasing={{0}: (6, {})} | custom-call | flops 21474836480 | bytes 25165824 | tf_op jit(solution)/shard_map/mlp/pallas_call | solution.py:495
  492.3 1.1 add_bitcast_fusion
  493.6 1.2 pad_maximum_fusion
  494.7 3.5 all-to-all-start.2
  498.7 16.9 %all-to-all-done.2 = f32[4,128,640]{2,1,0:T(8,128)S(1)} async-done(((f32[4,128,640]{2,1,0:T(8,128)}), f32[4,128,640]{2,1,0:T(8,128)S(1)}, u32[]{:S(2)}, u32[]{:S(2)}) %all-to-all-start.2) | async-done | bytes 1310752 | tf_op jit(solution)/shard_map/all_to_all | solution.py:528
  515.7 17.0 %all_to_all.20 = f32[8,17,640]{2,1,0:T(8,128)S(1)} all-to-all(f32[8,17,640]{2,1,0:T(8,128)S(1)} %pad_maximum_fusion.1), channel_id=1, replica_groups=mesh['lat'=4,'grp'=8] {'grp'}, dimensions={0} | all-to-all | bytes 696320 | tf_op jit(solution)/shard_map/all_to_all | solution.py:528
  532.7 0.6 slice_reduce_fusion
  534.1 0.7 copy.62
  (52 shorter events, 2.9 us)
Async XLA Ops:
  2.9 13.6 %collective-permute-start = (f32[1,4,6]{0,1,2:T(4,128)S(1)}, f32[1,4,6]{0,1,2:T(4,128)S(1)}, u32[]{:S(2)}, u32[]{:S(2)}) collective-permute-start(f32[1,4,6]{0,1,2:T(4,128)S(1)} %get-tuple-element.66), channel_id=1, source_target_pairs={{0,8},{8,16},{16,24},{1,9},{9,17},{17,25},{2,10},{10,18},{18,26},{... | collective-permute-start | bytes 296 | tf_op jit(solution)/shard_map/ppermute | solution.py:542
  5.2 11.3 %collective-permute-start.1 = (f32[1,4,6]{0,1,2:T(4,128)S(1)}, f32[1,4,6]{0,1,2:T(4,128)S(1)}, u32[]{:S(2)}, u32[]{:S(2)}) collective-permute-start(f32[1,4,6]{0,1,2:T(4,128)S(1)} %get-tuple-element.67), channel_id=1, source_target_pairs={{8,0},{16,8},{24,16},{9,1},{17,9},{25,17},{10,2},{18,10},{26,18},{... | collective-permute-start | bytes 296 | tf_op jit(solution)/shard_map/ppermute | solution.py:543
  9.3 10.1 %collective-permute-start.3 = (bf16[32,16,1024]{2,1,0:T(8,128)(2,1)}, bf16[32,16,1024]{2,1,0:T(8,128)(2,1)S(1)}, u32[]{:S(2)}, u32[]{:S(2)}) collective-permute-start(bf16[32,16,1024]{2,1,0:T(8,128)(2,1)} %get-tuple-element.62), channel_id=1, source_target_pairs={{8,0},{16,8},{24,16},{9,1},{17,9},{25,17},{10,2},{18,10},{26,18},{... | collective-permute-start | bytes 3145736 | tf_op jit(solution)/shard_map/ppermute | solution.py:543
  10.6 8.9 %collective-permute-start.2 = (bf16[32,16,1024]{2,1,0:T(8,128)(2,1)S(1)}, bf16[32,16,1024]{2,1,0:T(8,128)(2,1)S(1)}, u32[]{:S(2)}, u32[]{:S(2)}) collective-permute-start(bf16[32,16,1024]{2,1,0:T(8,128)(2,1)S(1)} %get-tuple-element.63), channel_id=1, source_target_pairs={{0,8},{8,16},{16,24},{1,9},{9,17},{17,25},{2,10},{10,18},{18,26},{... | collective-permute-start | bytes 3145736 | tf_op jit(solution)/shard_map/ppermute | solution.py:542
  19.5 0.9 copy-start.3
  71.7 24.0 %copy-start.2 = (s32[128,384]{1,0:T(8,128)S(1)}, s32[128,384]{1,0:T(8,128)}, u32[]{:S(2)}) copy-start(s32[128,384]{1,0:T(8,128)} %constant.38.clone.grid_ref) | copy-start | bytes 589828
  71.7 181.7 %all-to-all-start = ((bf16[8,16,32,1024]{3,2,1,0:T(8,128)(2,1)}), bf16[8,16,32,1024]{3,2,1,0:T(8,128)(2,1)}, u32[]{:S(2)}, u32[]{:S(2)}) async-start(bf16[8,16,32,1024]{3,2,1,0:T(8,128)(2,1)} %get-tuple-element.19), calls=%async_computation | async-start | bytes 16777216 | tf_op jit(solution)/shard_map/all_to_all | solution.py:566
  79.4 14.2 %collective-permute-start.5 = (bf16[32,16,1024]{2,1,0:T(8,128)(2,1)S(1)}, bf16[32,16,1024]{2,1,0:T(8,128)(2,1)S(1)}, u32[]{:S(2)}, u32[]{:S(2)}) collective-permute-start(bf16[32,16,1024]{2,1,0:T(8,128)(2,1)S(1)} %get-tuple-element.60), channel_id=1, source_target_pairs={{8,0},{16,8},{24,16},{9,1},{17,9},{25,17},{10,2},{18,10},{26,18},{... | collective-permute-start | bytes 3145736 | tf_op jit(solution)/shard_map/ppermute | solution.py:543
  80.7 15.0 %collective-permute-start.4 = (bf16[32,16,1024]{2,1,0:T(8,128)(2,1)S(1)}, bf16[32,16,1024]{2,1,0:T(8,128)(2,1)S(1)}, u32[]{:S(2)}, u32[]{:S(2)}) collective-permute-start(bf16[32,16,1024]{2,1,0:T(8,128)(2,1)S(1)} %get-tuple-element.61), channel_id=1, source_target_pairs={{0,8},{8,16},{16,24},{1,9},{9,17},{17,25},{2,10},{10,18},{18,26},{... | collective-permute-start | bytes 3145736 | tf_op jit(solution)/shard_map/ppermute | solution.py:542
  253.4 12.5 %copy-start.4 = (f32[512]{0:T(512)S(1)}, f32[512]{0:T(512)}, u32[]{:S(2)}) copy-start(f32[512]{0:T(512)} %param.14) | copy-start | bytes 6148
  253.4 12.7 %copy-start = (bf16[256,512]{1,0:T(8,128)(2,1)S(1)}, bf16[256,512]{1,0:T(8,128)(2,1)}, u32[]{:S(2)}) copy-start(bf16[256,512]{1,0:T(8,128)(2,1)} %refs_2_.3) | copy-start | bytes 786436
  253.4 12.8 %copy-start.1 = (bf16[512,256]{1,0:T(8,128)(2,1)S(1)}, bf16[512,256]{1,0:T(8,128)(2,1)}, u32[]{:S(2)}) copy-start(bf16[512,256]{1,0:T(8,128)(2,1)} %refs_5_.3) | copy-start | bytes 786436
  253.4 197.1 %all-to-all-start.1 = ((bf16[8,16,32,1024]{3,2,1,0:T(8,128)(2,1)}), bf16[8,16,32,1024]{3,2,1,0:T(8,128)(2,1)}, u32[]{:S(2)}, u32[]{:S(2)}) async-start(bf16[8,16,32,1024]{3,2,1,0:T(8,128)(2,1)} %get-tuple-element.20), calls=%async_computation.1 | async-start | bytes 16777216 | tf_op jit(solution)/shard_map/all_to_all | solution.py:566
  494.7 20.8 %all-to-all-start.2 = ((f32[4,128,640]{2,1,0:T(8,128)}), f32[4,128,640]{2,1,0:T(8,128)S(1)}, u32[]{:S(2)}, u32[]{:S(2)}) async-start(f32[4,128,640]{2,1,0:T(8,128)} %bitcast.8), calls=%async_computation.2 | async-start | bytes 2621440 | tf_op jit(solution)/shard_map/all_to_all | solution.py:528
